TPU v7x, 32 devices: a whole 2x2x4 slice. The times are simulated.
32 devices in a mesh: ctx: 8 (over z, x), tp: 4 (over y, core).
Axes of the slice: x: 2, y: 2, z: 4, core: 2. Of those that a mesh axis runs over, the one named last changes fastest.
Arguments:
- queries: bfloat16 [256, 8192], P('ctx', 'tp'), may hold values from -6 to 6
- cache_keys: bfloat16 [32768, 1024], P('ctx', 'tp'), may hold values from -18 to 18
- cache_values: bfloat16 [32768, 1024], P('ctx', 'tp'), may hold values from -6 to 6
- span_keys: bfloat16 [256, 1024], P('ctx', 'tp'), may hold values from -24 to 24
- span_values: bfloat16 [256, 1024], P('ctx', 'tp'), may hold values from -6 to 6
- out_weight: bfloat16 [8192, 8192], P('tp', 'ctx'), may hold values from -0.0625 to 0.0625
- residual: bfloat16 [256, 8192], P('tp', 'ctx'), may hold values from -72 to 72
- norm_gain: bfloat16 [8192], P('ctx'), may hold values from 0.5 to 1.5
- head_weight: bfloat16 [8192, 128256], P(None, ('ctx', 'tp')), may hold values from -0.198873782 to 0.198873782
- targets: int32 [256], replicated, may hold values from 0 to 128255
- window_lengths: int32 [4], replicated, may hold values from 1 to 128, 256 in all
Outputs:
- token_logprob: float32 [256], P('ctx')
- window_means: float32 [4], replicated
Inputs may be any that keep to these rules, and one draw needn't show every extreme that they name: `window_lengths`: the 4 lengths sum to 256.
All inputs are finite; a program needn't handle non-finite values.
Results may differ from a plain program's by a relative error of at most 0.0025.
Values may be sent and summed in bfloat16 or wider, within the bound.
A program may use at most 128 MiB of HBM per device.

v0:
```python
import jax
import jax.numpy as jnp
from jax import lax
from jax.sharding import PartitionSpec as P

D = 8192
HEADS = 64
KV_HEADS = 8
HD = 128


EPSILON = 1e-05
NEGATIVE = -1e30


def fold_block(state, scores, value_rows):
    row_max, row_sum, weighted = state
    new_max = jnp.maximum(row_max, jnp.max(scores, axis=1))
    fading = jnp.exp(row_max - new_max)
    weights = jnp.exp(scores - new_max[:, None])
    row_sum = row_sum * fading + jnp.sum(weights, axis=1)
    weighted = weighted * fading[:, None] + jnp.dot(
        weights.astype(jnp.bfloat16), value_rows, preferred_element_type=jnp.float32
    )
    return (new_max, row_sum, weighted)


def partial_head(
    query_rows, cache_part, value_part, fresh_keys, fresh_values, first_token, span_total
):
    row_count = query_rows.shape[0]
    scaling = HD ** (-0.5)
    block_size = min(1024, cache_part.shape[0])
    block_count = cache_part.shape[0] // block_size
    key_blocks = cache_part.reshape(block_count, block_size, HD)
    value_blocks = value_part.reshape(block_count, block_size, HD)

    def advance(state, block_pair):
        scores = jnp.dot(query_rows, block_pair[0].T, preferred_element_type=jnp.float32) * scaling
        return (fold_block(state, scores, block_pair[1]), None)

    start_state = (
        jnp.full((row_count,), NEGATIVE, jnp.float32),
        jnp.zeros((row_count,), jnp.float32),
        jnp.zeros((row_count, HD), jnp.float32),
    )
    state, unused = lax.scan(advance, start_state, (key_blocks, value_blocks))
    scores = jnp.dot(query_rows, fresh_keys.T, preferred_element_type=jnp.float32) * scaling
    token_of_row = jnp.arange(row_count, dtype=jnp.int32) % span_total
    key_token = first_token + jnp.arange(fresh_keys.shape[0], dtype=jnp.int32)
    scores = jnp.where(token_of_row[:, None] >= key_token[None, :], scores, NEGATIVE)
    return fold_block(state, scores, fresh_values)


def local(
    queries,
    cache_keys,
    cache_values,
    span_keys,
    span_values,
    out_weight,
    residual,
    norm_gain,
    head_weight,
    targets,
    window_lengths,
):
    ctx_rank = lax.axis_index("ctx")
    span_dev = queries.shape[0]
    group_size = HEADS // KV_HEADS
    kv_local = cache_keys.shape[1] // HD
    heads_local = kv_local * group_size
    query_all = lax.all_gather(queries, "ctx", axis=0, tiled=True)
    span_total = query_all.shape[0]
    query_heads = (
        query_all.reshape(span_total, kv_local, group_size, HD)
        .transpose(1, 2, 0, 3)
        .reshape(kv_local, group_size * span_total, HD)
    )
    first_token = ctx_rank * span_dev
    maxima = []
    totals = []
    weighted_rows = []
    for head_index in range(kv_local):
        lower = head_index * HD
        row_max, row_sum, weighted = partial_head(
            query_heads[head_index],
            cache_keys[:, lower : lower + HD],
            cache_values[:, lower : lower + HD],
            span_keys[:, lower : lower + HD],
            span_values[:, lower : lower + HD],
            first_token,
            span_total,
        )
        maxima.append(row_max)
        totals.append(row_sum)
        weighted_rows.append(weighted)
    part_max = (
        jnp.stack(maxima)
        .reshape(kv_local, group_size, span_total)
        .transpose(2, 0, 1)
        .reshape(span_total, heads_local)
    )
    part_sum = (
        jnp.stack(totals)
        .reshape(kv_local, group_size, span_total)
        .transpose(2, 0, 1)
        .reshape(span_total, heads_local)
    )
    part_weighted = (
        jnp.stack(weighted_rows)
        .reshape(kv_local, group_size, span_total, HD)
        .transpose(2, 0, 1, 3)
        .reshape(span_total, heads_local * HD)
    )
    pieces = (
        lax.all_to_all(
            part_max[None].astype(jnp.bfloat16), "ctx", split_axis=1, concat_axis=0, tiled=True
        ).astype(jnp.float32),
        lax.all_to_all(
            part_sum[None].astype(jnp.bfloat16), "ctx", split_axis=1, concat_axis=0, tiled=True
        ).astype(jnp.float32),
        lax.all_to_all(
            part_weighted[None].astype(jnp.bfloat16), "ctx", split_axis=1, concat_axis=0, tiled=True
        ).astype(jnp.float32),
    )
    source_count = pieces[0].shape[0]
    row_max = jnp.max(pieces[0], axis=0)
    fading = jnp.exp(pieces[0] - row_max[None])
    row_sum = jnp.sum(pieces[1] * fading, axis=0)
    weighted = jnp.sum(
        pieces[2].reshape(source_count, span_dev, heads_local, HD) * fading[:, :, :, None], axis=0
    )
    attended_own = (
        (weighted / row_sum[:, :, None]).reshape(span_dev, heads_local * HD).astype(jnp.bfloat16)
    )
    attended_all = lax.all_gather(attended_own, "ctx", axis=0, tiled=True)
    projected = lax.psum_scatter(
        jnp.dot(attended_all, out_weight, preferred_element_type=jnp.float32).astype(jnp.bfloat16),
        "tp",
        scatter_dimension=0,
        tiled=True,
    ).astype(jnp.float32)
    stream = residual.astype(jnp.float32) + projected
    squares = lax.psum(jnp.sum(stream * stream, axis=1), "ctx")
    scaled = lax.rsqrt(squares / D + EPSILON)
    normed_part = (stream * scaled[:, None] * norm_gain.astype(jnp.float32)[None, :]).astype(
        jnp.bfloat16
    )
    normed_rows = lax.all_gather(normed_part, "ctx", axis=1, tiled=True)
    logits = jnp.dot(
        lax.all_gather(normed_rows, "tp", axis=0, tiled=True),
        head_weight,
        preferred_element_type=jnp.float32,
    )
    vocab_dev = head_weight.shape[1]
    vocab_start = lax.axis_index(("ctx", "tp")) * vocab_dev
    columns = vocab_start + jnp.arange(vocab_dev, dtype=jnp.int32)
    target_part = jnp.sum(jnp.where(targets[:, None] == columns[None, :], logits, 0.0), axis=1)
    local_max = jnp.max(logits, axis=1)
    global_max = lax.pmax(local_max, ("ctx", "tp"))
    exp_part = jnp.sum(jnp.exp(logits - global_max[:, None]), axis=1)
    exp_total, target_logit = lax.psum((exp_part, target_part), ("ctx", "tp"))
    token_logprob = target_logit - (global_max + jnp.log(exp_total))
    window_ends = jnp.cumsum(window_lengths)
    window_starts = window_ends - window_lengths
    positions = jnp.arange(span_total, dtype=jnp.int32)
    member = (
        (positions[None, :] >= window_starts[:, None]) & (positions[None, :] < window_ends[:, None])
    ).astype(jnp.float32)
    window_sums = jnp.dot(member, token_logprob, precision=lax.Precision.HIGHEST)
    window_means = window_sums / window_lengths.astype(jnp.float32)
    own_logprob = lax.dynamic_slice_in_dim(token_logprob, first_token, span_dev, 0)
    return (own_logprob, window_means)


def solution(mesh):
    in_specs = (
        P("ctx", "tp"),
        P("ctx", "tp"),
        P("ctx", "tp"),
        P("ctx", "tp"),
        P("ctx", "tp"),
        P("tp", "ctx"),
        P("tp", "ctx"),
        P("ctx"),
        P(None, ("ctx", "tp")),
        P(),
        P(),
    )
    out_specs = (P("ctx"), P())
    return jax.shard_map(local, mesh=mesh, in_specs=in_specs, out_specs=out_specs, check_vma=False)
```

profile of v0, /device:TPU:0, one launch (start us, length us, event | category | flops | bytes accessed | tf_op | source)
XLA Modules:
  0.0 509.2 jit_solution(16543837687010542798)
XLA Ops:
  14.0 39.0 %all-gather.5.cloned.1.call-done = bf16[256,2048]{1,0:T(8,128)(2,1)} async-done(((bf16[32,2048]{1,0:T(8,128)(2,1)}), bf16[256,2048]{1,0:T(8,128)(2,1)}) %all-gather.5.cloned.1.call-update) | async-done | bytes 1048592 | tf_op jit(solution)/shard_map/all_gather | solution.py:73
  54.9 56.6 %while.31 = (s32[]{:T(128)}, f32[2048]{0:T(1024)S(1)}, f32[2048]{0:T(1024)S(1)}, f32[2048,128]{1,0:T(8,128)S(1)}, bf16[4,1024,128]{2,1,0:T(8,128)(2,1)}, /*index...) while((s32[]{:T(128)}, f32[2048]{0:T(1024)S(1)}, ...), condition=%wide.region_8.9_spmd.clone, body=%wide.region_5.8_spmd.clone.sunk | while | flops 1091315712 | bytes 61997204 | solution.py:47
  54.9 5.4 %multiply_reduce_fusion.8 = (f32[2048]{0:T(1024)S(1)}, f32[1024,2048]{1,0:T(8,128)}) fusion(bf16[2048,128]{1,0:T(8,128)(2,1)S(1)} %get-tuple-element.321, bf16[4,1024,128]{2,1,0:T(8,128)(2,1)} %get-tuple-element.320, s32[]{:T(128)S(6)} %copy.70), kind=kOutput, calls=%fused_computation.22.clone.1 | convolution fusion | flops 541063168 | bytes 9183236 | tf_op jit(solution)/shard_map/while/body/eval_jaxpr/dot_general | solution.py:39
  60.3 4.9 fusion.98
  69.0 5.4 %multiply_reduce_fusion.8 = (f32[2048]{0:T(1024)S(1)}, f32[1024,2048]{1,0:T(8,128)}) fusion(bf16[2048,128]{1,0:T(8,128)(2,1)S(1)} %get-tuple-element.321, bf16[4,1024,128]{2,1,0:T(8,128)(2,1)} %get-tuple-element.320, s32[]{:T(128)S(6)} %copy.70), kind=kOutput, calls=%fused_computation.22.clone.1 | convolution fusion | flops 541063168 | bytes 9183236 | tf_op jit(solution)/shard_map/while/body/eval_jaxpr/dot_general | solution.py:39
  74.5 4.9 fusion.98
  83.2 5.4 %multiply_reduce_fusion.8 = (f32[2048]{0:T(1024)S(1)}, f32[1024,2048]{1,0:T(8,128)}) fusion(bf16[2048,128]{1,0:T(8,128)(2,1)S(1)} %get-tuple-element.321, bf16[4,1024,128]{2,1,0:T(8,128)(2,1)} %get-tuple-element.320, s32[]{:T(128)S(6)} %copy.70), kind=kOutput, calls=%fused_computation.22.clone.1 | convolution fusion | flops 541063168 | bytes 9183236 | tf_op jit(solution)/shard_map/while/body/eval_jaxpr/dot_general | solution.py:39
  88.6 4.9 fusion.98
  97.3 5.4 %multiply_reduce_fusion.8 = (f32[2048]{0:T(1024)S(1)}, f32[1024,2048]{1,0:T(8,128)}) fusion(bf16[2048,128]{1,0:T(8,128)(2,1)S(1)} %get-tuple-element.321, bf16[4,1024,128]{2,1,0:T(8,128)(2,1)} %get-tuple-element.320, s32[]{:T(128)S(6)} %copy.70), kind=kOutput, calls=%fused_computation.22.clone.1 | convolution fusion | flops 541063168 | bytes 9183236 | tf_op jit(solution)/shard_map/while/body/eval_jaxpr/dot_general | solution.py:39
  102.8 4.9 fusion.98
  112.1 56.6 %while.30 = (s32[]{:T(128)}, f32[2048]{0:T(1024)S(1)}, f32[2048]{0:T(1024)S(1)}, f32[2048,128]{1,0:T(8,128)S(1)}, bf16[4,1024,128]{2,1,0:T(8,128)(2,1)}, /*index...) while((s32[]{:T(128)}, f32[2048]{0:T(1024)S(1)}, ...), condition=%wide.region_3.4_spmd.clone, body=%wide.region_0.3_spmd.clone.sunk | while | flops 1091315712 | bytes 61997204 | solution.py:47
  112.1 5.4 %multiply_reduce_fusion.7 = (f32[2048]{0:T(1024)S(1)}, f32[1024,2048]{1,0:T(8,128)}) fusion(bf16[2048,128]{1,0:T(8,128)(2,1)S(1)} %get-tuple-element.348, bf16[4,1024,128]{2,1,0:T(8,128)(2,1)} %get-tuple-element.347, s32[]{:T(128)S(6)} %copy.82), kind=kOutput, calls=%fused_computation.1.clone.1 | convolution fusion | flops 541063168 | bytes 9183236 | tf_op jit(solution)/shard_map/while/body/eval_jaxpr/dot_general | solution.py:39
  117.5 4.9 fusion.92
  126.2 5.4 %multiply_reduce_fusion.7 = (f32[2048]{0:T(1024)S(1)}, f32[1024,2048]{1,0:T(8,128)}) fusion(bf16[2048,128]{1,0:T(8,128)(2,1)S(1)} %get-tuple-element.348, bf16[4,1024,128]{2,1,0:T(8,128)(2,1)} %get-tuple-element.347, s32[]{:T(128)S(6)} %copy.82), kind=kOutput, calls=%fused_computation.1.clone.1 | convolution fusion | flops 541063168 | bytes 9183236 | tf_op jit(solution)/shard_map/while/body/eval_jaxpr/dot_general | solution.py:39
  131.7 4.9 fusion.92
  140.4 5.4 %multiply_reduce_fusion.7 = (f32[2048]{0:T(1024)S(1)}, f32[1024,2048]{1,0:T(8,128)}) fusion(bf16[2048,128]{1,0:T(8,128)(2,1)S(1)} %get-tuple-element.348, bf16[4,1024,128]{2,1,0:T(8,128)(2,1)} %get-tuple-element.347, s32[]{:T(128)S(6)} %copy.82), kind=kOutput, calls=%fused_computation.1.clone.1 | convolution fusion | flops 541063168 | bytes 9183236 | tf_op jit(solution)/shard_map/while/body/eval_jaxpr/dot_general | solution.py:39
  145.8 4.9 fusion.92
  154.5 5.4 %multiply_reduce_fusion.7 = (f32[2048]{0:T(1024)S(1)}, f32[1024,2048]{1,0:T(8,128)}) fusion(bf16[2048,128]{1,0:T(8,128)(2,1)S(1)} %get-tuple-element.348, bf16[4,1024,128]{2,1,0:T(8,128)(2,1)} %get-tuple-element.347, s32[]{:T(128)S(6)} %copy.82), kind=kOutput, calls=%fused_computation.1.clone.1 | convolution fusion | flops 541063168 | bytes 9183236 | tf_op jit(solution)/shard_map/while/body/eval_jaxpr/dot_general | solution.py:39
  160.0 4.9 fusion.92
  186.6 6.8 %reduce.9 = bf16[256,2048]{1,0:T(8,128)(2,1)S(1)} reduce(bf16[256,1,2048]{2,1,0:T(2,128)(2,1)S(1)} %bitcast.89, bf16[]{:T(256)} %broadcast.154), dimensions={1}, to_apply=%bitcast.52.reduce_sub_computation | reduce | bytes 2097154
  195.0 5.9 %all-to-all-start = ((bf16[8,2,32768]{2,1,0:T(2,128)(2,1)}), bf16[8,2,32768]{2,1,0:T(2,128)(2,1)S(1)}, u32[]{:S(2)}, u32[]{:S(2)}) async-start(bf16[8,2,32768]{2,1,0:T(2,128)(2,1)} %reshape.197), calls=%async_computation | async-start | bytes 2097152 | tf_op jit(solution)/shard_map/all_to_all | solution.py:123
  202.1 22.5 %all-to-all-done = bf16[8,2,32768]{2,1,0:T(2,128)(2,1)S(1)} async-done(((bf16[8,2,32768]{2,1,0:T(2,128)(2,1)}), bf16[8,2,32768]{2,1,0:T(2,128)(2,1)S(1)}, u32[]{:S(2)}, u32[]{:S(2)}) %all-to-all-start) | async-done | bytes 1048608 | tf_op jit(solution)/shard_map/all_to_all | solution.py:123
  229.5 39.1 %all-gather.7.cloned.1.call-done = bf16[256,2048]{1,0:T(8,128)(2,1)} async-done(((bf16[32,2048]{1,0:T(8,128)(2,1)}), bf16[256,2048]{1,0:T(8,128)(2,1)}) %all-gather.7.cloned.1.call-update) | async-done | bytes 1048592 | tf_op jit(solution)/shard_map/all_gather | solution.py:137
  268.6 4.6 convolution_convert_fusion
  273.3 20.5 %reduce-scatter.2.cloned.1.call-done = bf16[64,1024]{1,0:T(8,128)(2,1)} async-done(((bf16[256,1024]{1,0:T(8,128)(2,1)}), bf16[64,1024]{1,0:T(8,128)(2,1)}) %reduce-scatter.2.cloned.1.call-update) | async-done | bytes 131088 | tf_op jit(solution)/shard_map/reduce_scatter | solution.py:138
  294.8 21.4 %psum.21 = f32[64]{0:T(128)S(1)} all-reduce(f32[64]{0:T(128)S(1)} %multiply_reduce_fusion.3), channel_id=1, replica_groups=mesh['ctx'=8,'tp'=4] {'ctx'}, use_global_device_ids=true, to_apply=%region_17.18 | all-reduce | flops 64 | bytes 512 | tf_op jit(solution)/shard_map/psum | solution.py:145
  317.9 36.6 %all-gather.9.cloned.1.call-done = bf16[64,8192]{1,0:T(8,128)(2,1)} async-done(((bf16[64,1024]{1,0:T(8,128)(2,1)}), bf16[64,8192]{1,0:T(8,128)(2,1)}) %all-gather.9.cloned.1.call-update) | async-done | bytes 1048592 | tf_op jit(solution)/shard_map/all_gather | solution.py:150
  354.8 34.5 %all-gather.11.cloned.1.call-done = bf16[256,8192]{1,0:T(8,128)(2,1)} async-done(((bf16[64,8192]{1,0:T(8,128)(2,1)}), bf16[256,8192]{1,0:T(8,128)(2,1)}) %all-gather.11.cloned.1.call-update) | async-done | bytes 4194320 | tf_op jit(solution)/shard_map/all_gather | solution.py:152
  389.3 27.9 %fusion.67 = (f32[256]{0:T(256)S(1)}, f32[256,4008]{0,1:T(8,128)}) fusion(bf16[256,8192]{1,0:T(8,128)(2,1)} %all-gather.11.cloned.1.call-done, bf16[8192,4008]{0,1:T(8,128)(2,1)} %param.23), kind=kOutput, calls=%fused_computation.105 | convolution fusion | flops 16811796480 | bytes 73966592 | tf_op jit(solution)/shard_map/dot_general | solution.py:151
  417.2 39.3 %pmax.7 = f32[256]{0:T(256)S(1)} all-reduce(f32[256]{0:T(256)S(1)} %get-tuple-element.194), channel_id=1, replica_groups=mesh['ctx'=8,'tp'=4] {'ctx','tp'}, use_global_device_ids=true, to_apply=%region_21.22 | all-reduce | flops 256 | bytes 2048 | tf_op jit(solution)/shard_map/pmax | solution.py:161
  456.5 3.9 exponential_reduce_fusion
  460.4 41.0 %all-reduce = (f32[256]{0:T(256)S(1)}, f32[256]{0:T(256)S(1)}) all-reduce(f32[256]{0:T(256)S(1)} %get-tuple-element.135, f32[256]{0:T(256)S(1)} %get-tuple-element.134), channel_id=1, replica_groups=mesh['ctx'=8,'tp'=4] {'ctx','tp'}, use_global_device_ids=true, to_apply=%region_19.20 | all-reduce | flops 512 | bytes 4096 | tf_op jit(solution)/shard_map/psum | solution.py:163
  (141 shorter events, 68.8 us)
Async XLA Ops:
  7.2 45.9 %all-gather.5.cloned.1.call-start = ((), (), s32[]{:S(2)}) async-start(), calls=%async_computation.4 | async-start | bytes 1179648 | tf_op jit(solution)/shard_map/all_gather | solution.py:73
  54.9 56.6 %copy-start.3 = (bf16[32,256]{1,0:T(8,128)(2,1)S(1)}, bf16[32,256]{1,0:T(8,128)(2,1)}, u32[]{:S(2)}) copy-start(bf16[32,256]{1,0:T(8,128)(2,1)} %param.18) | copy-start | bytes 49156
  60.3 5.8 %copy-start = (f32[1024,2048]{1,0:T(8,128)S(1)}, f32[1024,2048]{1,0:T(8,128)}, u32[]{:S(2)}) copy-start(f32[1024,2048]{1,0:T(8,128)} %get-tuple-element.295) | copy-start | bytes 25165828 | tf_op jit(solution)/shard_map/while
  74.5 5.8 %copy-start = (f32[1024,2048]{1,0:T(8,128)S(1)}, f32[1024,2048]{1,0:T(8,128)}, u32[]{:S(2)}) copy-start(f32[1024,2048]{1,0:T(8,128)} %get-tuple-element.295) | copy-start | bytes 25165828 | tf_op jit(solution)/shard_map/while
  88.6 5.8 %copy-start = (f32[1024,2048]{1,0:T(8,128)S(1)}, f32[1024,2048]{1,0:T(8,128)}, u32[]{:S(2)}) copy-start(f32[1024,2048]{1,0:T(8,128)} %get-tuple-element.295) | copy-start | bytes 25165828 | tf_op jit(solution)/shard_map/while
  102.7 5.8 %copy-start = (f32[1024,2048]{1,0:T(8,128)S(1)}, f32[1024,2048]{1,0:T(8,128)}, u32[]{:S(2)}) copy-start(f32[1024,2048]{1,0:T(8,128)} %get-tuple-element.295) | copy-start | bytes 25165828 | tf_op jit(solution)/shard_map/while
  112.1 62.8 %copy-start.4 = (bf16[32,256]{1,0:T(8,128)(2,1)S(1)}, bf16[32,256]{1,0:T(8,128)(2,1)}, u32[]{:S(2)}) copy-start(bf16[32,256]{1,0:T(8,128)(2,1)} %param.19) | copy-start | bytes 49156
  117.5 5.8 %copy-start.1 = (f32[1024,2048]{1,0:T(8,128)S(1)}, f32[1024,2048]{1,0:T(8,128)}, u32[]{:S(2)}) copy-start(f32[1024,2048]{1,0:T(8,128)} %get-tuple-element.284) | copy-start | bytes 25165828 | tf_op jit(solution)/shard_map/while
  131.7 5.8 %copy-start.1 = (f32[1024,2048]{1,0:T(8,128)S(1)}, f32[1024,2048]{1,0:T(8,128)}, u32[]{:S(2)}) copy-start(f32[1024,2048]{1,0:T(8,128)} %get-tuple-element.284) | copy-start | bytes 25165828 | tf_op jit(solution)/shard_map/while
  145.8 5.8 %copy-start.1 = (f32[1024,2048]{1,0:T(8,128)S(1)}, f32[1024,2048]{1,0:T(8,128)}, u32[]{:S(2)}) copy-start(f32[1024,2048]{1,0:T(8,128)} %get-tuple-element.284) | copy-start | bytes 25165828 | tf_op jit(solution)/shard_map/while
  160.0 5.8 %copy-start.1 = (f32[1024,2048]{1,0:T(8,128)S(1)}, f32[1024,2048]{1,0:T(8,128)}, u32[]{:S(2)}) copy-start(f32[1024,2048]{1,0:T(8,128)} %get-tuple-element.284) | copy-start | bytes 25165828 | tf_op jit(solution)/shard_map/while
  171.3 9.9 %all-to-all-start.2 = ((bf16[8,2,256]{2,1,0:T(2,128)(2,1)}), bf16[8,2,256]{2,1,0:T(2,128)(2,1)S(1)}, u32[]{:S(2)}, u32[]{:S(2)}) async-start(bf16[8,2,256]{2,1,0:T(2,128)(2,1)} %reshape.201), calls=%async_computation.2 | async-start | bytes 16384 | tf_op jit(solution)/shard_map/all_to_all | solution.py:120
  181.2 13.8 %all-to-all-start.1 = ((bf16[8,2,256]{2,1,0:T(2,128)(2,1)}), bf16[8,2,256]{2,1,0:T(2,128)(2,1)S(1)}, u32[]{:S(2)}, u32[]{:S(2)}) async-start(bf16[8,2,256]{2,1,0:T(2,128)(2,1)} %reshape.199), calls=%async_computation.1 | async-start | bytes 16384 | tf_op jit(solution)/shard_map/all_to_all | solution.py:117
  195.0 29.6 %all-to-all-start = ((bf16[8,2,32768]{2,1,0:T(2,128)(2,1)}), bf16[8,2,32768]{2,1,0:T(2,128)(2,1)S(1)}, u32[]{:S(2)}, u32[]{:S(2)}) async-start(bf16[8,2,32768]{2,1,0:T(2,128)(2,1)} %reshape.197), calls=%async_computation | async-start | bytes 2097152 | tf_op jit(solution)/shard_map/all_to_all | solution.py:123
  201.0 67.6 %all-gather.7.cloned.1.call-start = ((), (), s32[]{:S(2)}) async-start(), calls=%async_computation.5 | async-start | bytes 1179648 | tf_op jit(solution)/shard_map/all_gather | solution.py:137
  225.6 47.6 %copy-start.5 = (bf16[1024]{0:T(1024)(128)(2,1)S(1)}, bf16[1024]{0:T(1024)(128)(2,1)}, u32[]{:S(2)}) copy-start(bf16[1024]{0:T(1024)(128)(2,1)} %param.22) | copy-start | bytes 6148
  225.6 68.1 %copy-start.2 = (bf16[64,1024]{1,0:T(8,128)(2,1)S(1)}, bf16[64,1024]{1,0:T(8,128)(2,1)}, u32[]{:S(2)}) copy-start(bf16[64,1024]{1,0:T(8,128)(2,1)} %param.21) | copy-start | bytes 393220
  225.7 128.9 %copy-start.7 = (s32[4]{0:T(128)S(1)}, s32[4]{0:T(128)}, u32[]{:S(2)}) copy-start(s32[4]{0:T(128)} %param.25) | copy-start | bytes 52
  229.4 64.4 %reduce-scatter.2.cloned.1.call-start = ((), (), s32[]{:S(2)}) async-start(), calls=%async_computation.6 | async-start | bytes 655360 | tf_op jit(solution)/shard_map/reduce_scatter | solution.py:138
  273.2 81.4 %all-gather.9.cloned.1.call-start = ((), (), s32[]{:S(2)}) async-start(), calls=%async_computation.7 | async-start | bytes 1179648 | tf_op jit(solution)/shard_map/all_gather | solution.py:150
  317.9 71.4 %all-gather.11.cloned.1.call-start = ((), (), s32[]{:S(2)}) async-start(), calls=%async_computation.8 | async-start | bytes 5242880 | tf_op jit(solution)/shard_map/all_gather | solution.py:152
  354.8 101.7 %copy-start.6 = (s32[256]{0:T(256)S(1)}, s32[256]{0:T(256)}, u32[]{:S(2)}) copy-start(s32[256]{0:T(256)} %param.24) | copy-start | bytes 3076
Sparse Core Ops, SparseCore 0:
  10.1 42.8 all-gather.4
  229.5 38.9 all-gather.6
  273.3 20.4 reduce-scatter.1
  318.0 36.4 all-gather.8
  356.0 33.2 all-gather.10
where the time goes:
time: 510 us; the launch traced here: 509 us
  waiting for transfers between devices  196 us (38%)
  matrix products  102 us (20%)
  blocking collectives  102 us (20%)
  other arithmetic  58.7 us (12%)
  local copies, waits for them, and re-layouts  23.6 us (5%)
  between operations  14.2 us (3%)
  starting transfers between devices  13.2 us (3%)
    dot_general x8, matrix products, advance(): jnp.dot(query_rows, block_pair[0].T, preferred_element_type=jnp.float32)  43.4 us
    psum x1, blocking collectives, local(): exp_total, target_logit = lax.psum((exp_part, target_part), ('ctx', 'tp'))  41 us
    reduce_sum x10, other arithmetic, fold_block(): row_sum = row_sum * fading + jnp.sum(weights, axis=1)  39.6 us
    pmax x1, blocking collectives, local(): global_max = lax.pmax(local_max, ('ctx', 'tp'))  39.3 us
    all_gather x1, waiting for transfers between devices, local(): attended_all = lax.all_gather(attended_own, 'ctx', axis=0, tiled=True)  39.1 us
    all_gather x1, waiting for transfers between devices, local(): query_all = lax.all_gather(queries, 'ctx', axis=0, tiled=True)  39 us
    all_gather x1, waiting for transfers between devices, local(): normed_rows = lax.all_gather(normed_part, 'ctx', axis=1, tiled=True)  36.6 us
    all_gather x1, waiting for transfers between devices, local(): lax.all_gather(normed_rows, 'tp', axis=0, tiled=True)  34.5 us
  transfers between devices with their start and end apart: 8, of which 7 were waited for; matrix products, arithmetic and copies ran while one was open for 4% of the time, Pallas kernels for 0%

commit v1 on v0

v1 whole, which is shorter than its diff:
```python
import functools

import jax
import jax.numpy as jnp
from jax import lax
from jax.experimental import pallas as pl
from jax.experimental.pallas import tpu as pltpu
from jax.sharding import PartitionSpec as P

HD = 128
GROUP = 8
EPSILON = 1e-05
NEGATIVE = -1e30
MESH = pl.DeviceIdType.MESH
F32 = jnp.float32
BF16 = jnp.bfloat16


def dot_nt(left, right):
    return lax.dot_general(
        left, right, (((1,), (1,)), ((), ())), preferred_element_type=F32
    )


def remote(src, dst, send_sem, recv_sem, device):
    return pltpu.make_async_remote_copy(
        src_ref=src,
        dst_ref=dst,
        send_sem=send_sem,
        recv_sem=recv_sem,
        device_id=device,
        device_id_type=MESH,
    )


def kernel(
    n_ctx,
    n_tp,
    slots,
    chunk,
    query_ref,
    key_ref,
    value_ref,
    fresh_key_ref,
    fresh_value_ref,
    residual_ref,
    gain_ref,
    target_ref,
    out_weight_ref,
    head_ref,
    result_ref,
    q_buf,
    o_send,
    s_send,
    o_buf,
    s_buf,
    a_buf,
    w_buf,
    p_send,
    p_buf,
    y_buf,
    sq_buf,
    column_buf,
    h_buf,
    acc,
    st_buf,
    q_ss,
    q_rs,
    o_ss,
    o_rs,
    s_ss,
    s_rs,
    a_ss,
    a_rs,
    p_ss,
    p_rs,
    y_ss,
    y_rs,
    sq_ss,
    sq_rs,
    st_ss,
    st_rs,
    w_sem,
    h_sem,
):
    c = lax.axis_index("ctx")
    t = lax.axis_index("tp")
    n_dev = n_ctx * n_tp
    me = c * n_tp + t
    kv_local = key_ref.shape[1] // HD
    span_dev = query_ref.shape[0]
    rows = span_dev * GROUP
    keys = key_ref.shape[0]
    tok_tp = residual_ref.shape[0]
    cols = residual_ref.shape[1]
    vocab_dev, width = head_ref.shape
    n_tokens = n_ctx * span_dev
    chunks = width // chunk
    half = tok_tp // 2
    scaling = HD ** (-0.5)

    def fetch(j, slot):
        return pltpu.make_async_copy(
            head_ref.at[:, pl.ds(pl.multiple_of(j * chunk, chunk), chunk)],
            h_buf.at[slot],
            h_sem.at[slot],
        )

    w_copy = pltpu.make_async_copy(out_weight_ref, w_buf, w_sem)
    w_copy.start()
    for j in range(slots):
        fetch(j, j).start()

    def other(step):
        index = lax.rem(me + step, n_dev)
        return (index // n_tp, lax.rem(index, n_tp))

    barrier = pltpu.get_barrier_semaphore()

    @pl.loop(1, n_dev)
    def _(step):
        pl.semaphore_signal(barrier, inc=1, device_id=other(step), device_id_type=MESH)

    pl.semaphore_wait(barrier, n_dev - 1)

    def peer(step):
        away = ((step + 1) // 2) * (2 * lax.rem(step, 2) - 1)
        return lax.rem(c + away + n_ctx, n_ctx)

    def query_copy(src_rank, dst):
        return remote(
            q_buf.at[src_rank], q_buf.at[src_rank], q_ss.at[dst], q_rs.at[src_rank], (dst, t)
        )

    def partial_copies(rank, dst):
        return (
            remote(o_send.at[dst], o_buf.at[rank], o_ss.at[dst], o_rs.at[rank], (dst, t)),
            remote(s_send.at[dst], s_buf.at[rank], s_ss.at[dst], s_rs.at[rank], (dst, t)),
        )

    for kv in range(kv_local):
        for g in range(GROUP):
            lo = (kv * GROUP + g) * HD
            q_buf[c, kv, g * span_dev : (g + 1) * span_dev, :] = query_ref[:, lo : lo + HD]

    @pl.loop(1, n_ctx)
    def _(step):
        query_copy(c, peer(step)).start()

    key_block = min(1024, keys)

    @pl.loop(0, n_ctx)
    def _(step):
        p = peer(step)

        @pl.when(step > 0)
        def _():
            query_copy(p, p).wait_recv()

        for kv in range(kv_local):
            lo = kv * HD
            q = q_buf[p, kv]
            row_max = None
            for b in range(keys // key_block + 1):
                if b < keys // key_block:
                    at = b * key_block
                    s = dot_nt(key_ref[at : at + key_block, lo : lo + HD], q)
                    v = value_ref[lo : lo + HD, at : at + key_block]
                else:
                    s = dot_nt(fresh_key_ref[:, lo : lo + HD], q)
                    j = lax.broadcasted_iota(jnp.int32, s.shape, 0)
                    token = lax.rem(
                        lax.broadcasted_iota(jnp.int32, s.shape, 1), span_dev
                    )
                    seen = (p * span_dev + token >= c * span_dev + j) & (j < span_dev)
                    s = jnp.where(seen, s, NEGATIVE)
                    v = fresh_value_ref[lo : lo + HD, :]
                top = jnp.max(s, axis=0, keepdims=True)
                if row_max is None:
                    new_max = top
                else:
                    new_max = jnp.maximum(row_max, top)
                w = jnp.exp((s - new_max) * scaling)
                part_sum = jnp.sum(w, axis=0, keepdims=True)
                part = jnp.dot(v, w.astype(BF16), preferred_element_type=F32)
                if row_max is None:
                    row_sum, weighted = part_sum, part
                else:
                    fading = jnp.exp((row_max - new_max) * scaling)
                    row_sum = row_sum * fading + part_sum
                    weighted = weighted * fading + part
                row_max = new_max
            o_send[p, kv] = (weighted / row_sum).astype(BF16)
            s_send[p, kv, 0:4, :] = jnp.broadcast_to(row_max * scaling, (4, rows))
            s_send[p, kv, 4:8, :] = jnp.broadcast_to(row_sum, (4, rows))

        @pl.when(step > 0)
        def _():
            for copy in partial_copies(c, p):
                copy.start()

    o_buf[c] = o_send[c]
    s_buf[c] = s_send[c]

    @pl.loop(1, n_ctx)
    def _(step):
        p = peer(step)
        query_copy(c, p).wait_send()
        for copy in partial_copies(p, p):
            copy.wait_send()
            copy.wait_recv()

    for kv in range(kv_local):
        tops = [s_buf[src, kv, 0:1, :] for src in range(n_ctx)]
        best = functools.reduce(jnp.maximum, tops)
        total = jnp.zeros((1, rows), F32)
        mixed = jnp.zeros((HD, rows), F32)
        for src in range(n_ctx):
            share = s_buf[src, kv, 4:5, :] * jnp.exp(tops[src] - best)
            total = total + share
            mixed = mixed + o_buf[src, kv].astype(F32) * share
        attended = (mixed / total).T.astype(BF16)
        for g in range(GROUP):
            lo = (kv * GROUP + g) * HD
            a_buf[c, :, lo : lo + HD] = attended[g * span_dev : (g + 1) * span_dev]

    def attended_copy(rank, dst):
        return remote(a_buf.at[rank], a_buf.at[rank], a_ss.at[dst], a_rs.at[rank], (dst, t))

    @pl.loop(1, n_ctx)
    def _(step):
        attended_copy(c, peer(step)).start()

    w_copy.wait()

    @pl.loop(1, n_ctx)
    def _(step):
        attended_copy(peer(step), peer(step)).wait_recv()

    tile = min(256, cols)
    for at in range(0, cols, tile):
        product = jnp.dot(
            a_buf[...].reshape(n_tokens, a_buf.shape[2]),
            w_buf[:, at : at + tile],
            preferred_element_type=F32,
        ).astype(BF16)
        p_send[:, :, at : at + tile] = product.reshape(n_tp, tok_tp, tile)

    def product_copy(rank, dst):
        return remote(p_send.at[dst], p_buf.at[rank], p_ss.at[dst], p_rs.at[rank], (c, dst))

    for step in range(1, n_tp):
        product_copy(t, lax.rem(t + step, n_tp)).start()
    p_buf[t] = p_send[t]
    for step in range(1, n_tp):
        dst = lax.rem(t + step, n_tp)
        product_copy(dst, dst).wait_recv()

    stream = residual_ref[...].astype(F32)
    for src in range(n_tp):
        stream = stream + p_buf[src].astype(F32)
    gained = (stream * gain_ref[...].astype(F32)).astype(BF16)
    y_buf[c, t, 0] = gained[:half]
    y_buf[c, t, 1] = gained[half:]
    squares = jnp.sum(stream * stream, axis=1, keepdims=True)
    column_buf[...] = jnp.zeros(column_buf.shape, F32)
    column_buf[pl.ds(pl.multiple_of(t * tok_tp, tok_tp), tok_tp), :] = jnp.broadcast_to(
        squares, (tok_tp, 128)
    )
    sq_buf[me] = column_buf[...].T[0:8]

    n_o = n_ctx // 2
    n_y = n_tp // 2
    o, i = c // 2, lax.rem(c, 2)
    y, k = t // 2, lax.rem(t, 2)
    sent = []

    def block_copy(cc, tt, h, device, sem):
        return remote(
            y_buf.at[cc, tt, h],
            y_buf.at[cc, tt, h],
            y_ss.at[sem],
            y_rs.at[(cc * n_tp + tt) * 2 + h],
            device,
        )

    def send(cc, tt, h, device):
        copy = block_copy(cc, tt, h, device, len(sent))
        copy.start()
        sent.append(copy)

    def arrive(cc, tt, h):
        block_copy(cc, tt, h, across, 0).wait_recv()

    across = (o * 2 + (1 - i), t)
    sides = [lax.rem(y + dy, n_y) * 2 + k for dy in range(1, n_y)]
    twin = (c, y * 2 + (1 - k))
    line = [lax.rem(o + dz, n_o) * 2 + i for dz in range(n_o)]
    line_across = [lax.rem(o + dz, n_o) * 2 + (1 - i) for dz in range(n_o)]

    def forward(cc):
        send(cc, t, 0, across)
        for side in sides:
            send(cc, t, 1, (c, side))
        for h in range(2):
            send(cc, t, h, twin)

    for cc in line[1:]:
        for h in range(2):
            send(c, t, h, (cc, t))
    forward(c)

    def square_copy(rank, step, device):
        return remote(sq_buf.at[rank], sq_buf.at[rank], sq_ss.at[step], sq_rs.at[rank], device)

    @pl.loop(1, n_dev)
    def _(step):
        square_copy(me, step, other(step)).start()

    for cc in line[1:]:
        for h in range(2):
            arrive(cc, t, h)
        forward(cc)
    for cc in line:
        for side in sides:
            send(cc, t, 0, (c, side))
        send(cc, t, 1, across)
    for dz in range(n_o):
        arrive(line_across[dz], t, 0)
        for side in sides:
            send(line_across[dz], t, 0, (c, side))
        send(line_across[dz], t, 0, twin)
        for side in sides:
            arrive(line[dz], side, 1)
            send(line[dz], side, 1, across)
            send(line[dz], side, 1, twin)
    for dz in range(n_o):
        for side in sides:
            arrive(line[dz], side, 0)
            send(line[dz], side, 0, twin)
        arrive(line_across[dz], t, 1)
        send(line_across[dz], t, 1, twin)
    for dz in range(n_o):
        for side in sides:
            for h in range(2):
                arrive(line_across[dz], side, h)
                send(line_across[dz], side, h, twin)
    for cc in range(n_ctx):
        for yy in range(n_y):
            for h in range(2):
                arrive(cc, yy * 2 + (1 - k), h)

    per_source = cols // chunk

    @pl.loop(0, chunks)
    def _(j):
        slot = lax.rem(j, slots)
        fetch(j, slot).wait()
        left = y_buf[
            j // per_source, :, :, :, pl.ds(pl.multiple_of(lax.rem(j, per_source) * chunk, chunk), chunk)
        ].reshape(n_tokens, chunk)
        for at in range(0, vocab_dev, 512):
            to = min(at + 512, vocab_dev)
            product = dot_nt(h_buf[slot, at:to, :], left)

            @pl.when(j == 0)
            def _():
                acc[at:to, :] = product

            @pl.when(j > 0)
            def _():
                acc[at:to, :] += product

        @pl.when(j + slots < chunks)
        def _():
            fetch(j + slots, slot).start()

    @pl.loop(1, n_dev)
    def _(step):
        square_copy(lax.rem(me + step, n_dev), step, other(step)).wait_recv()

    vocab_start = me * vocab_dev
    total = sq_buf[0, 0:1]
    for rank in range(1, n_dev):
        total = total + sq_buf[rank, 0:1]
    scale = lax.rsqrt(total / width + EPSILON)
    top = jnp.max(acc[...] * scale, axis=0, keepdims=True)
    mass = jnp.zeros((1, n_tokens), F32)
    mark = jnp.zeros((1, n_tokens), F32)
    for at in range(0, vocab_dev, 512):
        to = min(at + 512, vocab_dev)
        logits = acc[at:to, :] * scale
        mass = mass + jnp.sum(jnp.exp(logits - top), axis=0, keepdims=True)
        entry = vocab_start + at + lax.broadcasted_iota(jnp.int32, logits.shape, 0)
        hit = target_ref[...] == entry
        mark = mark + jnp.sum(jnp.where(hit, logits, 0.0), axis=0, keepdims=True)
    st_buf[me, 0:2, :] = jnp.broadcast_to(top, (2, n_tokens))
    st_buf[me, 2:4, :] = jnp.broadcast_to(mass, (2, n_tokens))
    st_buf[me, 4:8, :] = jnp.broadcast_to(mark, (4, n_tokens))

    def stat_copy(rank, step, device):
        return remote(st_buf.at[rank], st_buf.at[rank], st_ss.at[step], st_rs.at[rank], device)

    @pl.loop(1, n_dev)
    def _(step):
        stat_copy(me, step, other(step)).start()

    for copy in sent:
        copy.wait_send()

    @pl.loop(1, n_ctx)
    def _(step):
        attended_copy(c, peer(step)).wait_send()

    for step in range(1, n_tp):
        product_copy(t, lax.rem(t + step, n_tp)).wait_send()

    @pl.loop(1, n_dev)
    def _(step):
        square_copy(me, step, other(step)).wait_send()
        stat_copy(me, step, other(step)).wait_send()
        stat_copy(lax.rem(me + step, n_dev), step, other(step)).wait_recv()

    tops = [st_buf[rank, 0:1, :] for rank in range(n_dev)]
    top = functools.reduce(jnp.maximum, tops)
    mass = jnp.zeros((1, n_tokens), F32)
    mark = jnp.zeros((1, n_tokens), F32)
    for rank in range(n_dev):
        mass = mass + st_buf[rank, 2:3, :] * jnp.exp(tops[rank] - top)
        mark = mark + st_buf[rank, 4:5, :]
    result_ref[...] = jnp.broadcast_to(mark - (top + jnp.log(mass)), result_ref.shape)


def local(
    n_ctx,
    n_tp,
    queries,
    cache_keys,
    cache_values,
    span_keys,
    span_values,
    out_weight,
    residual,
    norm_gain,
    head_weight,
    targets,
    window_lengths,
):
    span_dev = queries.shape[0]
    kv_local = cache_keys.shape[1] // HD
    rows = GROUP * span_dev
    span_total = span_dev * n_ctx
    n_dev = n_ctx * n_tp
    heads_width = queries.shape[1]
    tok_tp, cols = residual.shape
    vocab_dev = head_weight.shape[1]
    chunk = min(512, cols)
    slots = 6
    padding = max(128 - span_dev, 0)
    fresh_keys = jnp.pad(span_keys, ((0, padding), (0, 0)))
    fresh_values = jnp.pad(span_values, ((0, padding), (0, 0))).T
    vmem = pl.BlockSpec(memory_space=pltpu.VMEM)
    hbm = pl.BlockSpec(memory_space=pl.ANY)
    dma = pltpu.SemaphoreType.DMA
    n_o, n_y = n_ctx // 2, n_tp // 2
    y_sends = (
        2 * (n_o - 1)
        + n_o * (1 + n_y)
        + (n_y - 1) * 3 * n_o
        + 2 * n_ctx * n_y
    )
    table = pl.pallas_call(
        functools.partial(kernel, n_ctx, n_tp, slots, chunk),
        out_shape=jax.ShapeDtypeStruct((8, span_total), F32),
        in_specs=[vmem] * 8 + [hbm] * 2,
        out_specs=vmem,
        scratch_shapes=[
            pltpu.VMEM((n_ctx, kv_local, rows, HD), BF16),
            pltpu.VMEM((n_ctx, kv_local, HD, rows), BF16),
            pltpu.VMEM((n_ctx, kv_local, 8, rows), F32),
            pltpu.VMEM((n_ctx, kv_local, HD, rows), BF16),
            pltpu.VMEM((n_ctx, kv_local, 8, rows), F32),
            pltpu.VMEM((n_ctx, span_dev, heads_width), BF16),
            pltpu.VMEM(out_weight.shape, BF16),
            pltpu.VMEM((n_tp, tok_tp, cols), BF16),
            pltpu.VMEM((n_tp, tok_tp, cols), BF16),
            pltpu.VMEM((n_ctx, n_tp, 2, tok_tp // 2, cols), BF16),
            pltpu.VMEM((n_dev, 8, span_total), F32),
            pltpu.VMEM((span_total, 128), F32),
            pltpu.VMEM((slots, vocab_dev, chunk), BF16),
            pltpu.VMEM((vocab_dev, span_total), F32),
            pltpu.VMEM((n_dev, 8, span_total), F32),
            dma((n_ctx,)),
            dma((n_ctx,)),
            dma((n_ctx,)),
            dma((n_ctx,)),
            dma((n_ctx,)),
            dma((n_ctx,)),
            dma((n_ctx,)),
            dma((n_ctx,)),
            dma((n_tp,)),
            dma((n_tp,)),
            dma((y_sends,)),
            dma((n_dev * 2,)),
            dma((n_dev,)),
            dma((n_dev,)),
            dma((n_dev,)),
            dma((n_dev,)),
            dma,
            dma((slots,)),
        ],
        compiler_params=pltpu.CompilerParams(
            collective_id=0, has_side_effects=True, vmem_limit_bytes=60 * 1024 * 1024
        ),
        name="score_span",
    )(
        queries,
        cache_keys,
        cache_values.T,
        fresh_keys,
        fresh_values,
        residual,
        norm_gain[None, :],
        targets[None, :],
        out_weight,
        head_weight.T,
    )
    token_logprob = table[0]
    window_ends = jnp.cumsum(window_lengths)
    window_starts = window_ends - window_lengths
    positions = jnp.arange(span_total, dtype=jnp.int32)
    member = (positions[None, :] >= window_starts[:, None]) & (
        positions[None, :] < window_ends[:, None]
    )
    window_sums = jnp.sum(jnp.where(member, token_logprob[None, :], 0.0), axis=1)
    window_means = window_sums / window_lengths.astype(F32)
    first_token = lax.axis_index("ctx") * span_dev
    own_logprob = lax.dynamic_slice_in_dim(token_logprob, first_token, span_dev, 0)
    return (own_logprob, window_means)


def solution(mesh):
    in_specs = (
        P("ctx", "tp"),
        P("ctx", "tp"),
        P("ctx", "tp"),
        P("ctx", "tp"),
        P("ctx", "tp"),
        P("tp", "ctx"),
        P("tp", "ctx"),
        P("ctx"),
        P(None, ("ctx", "tp")),
        P(),
        P(),
    )
    out_specs = (P("ctx"), P())
    body = functools.partial(local, mesh.shape["ctx"], mesh.shape["tp"])
    return jax.shard_map(body, mesh=mesh, in_specs=in_specs, out_specs=out_specs, check_vma=False)
```

time: 510 us -> 210 us (0.41)
  Pallas kernels: 0 us -> 200 us
  waiting for transfers between devices: 196 us -> 0 us
  matrix products: 102 us -> 0 us
  blocking collectives: 102 us -> 0 us
  other arithmetic: 58.7 us -> 0.89 us
  local copies, waits for them, and re-layouts: 23.6 us -> 7.4 us
  between operations: 14.2 us -> 0.68 us
  starting transfers between devices: 13.2 us -> 0 us
    pallas_call x0 -> x1, Pallas kernels: none -> 200 us  [local(): pl.pallas_call(functools.partial(kernel, n_ctx, n_tp, slots, chunk), out_...]
    all_gather x4 -> x0, waiting for transfers between devices: 149 us -> none  [the longest x1 39.1 us: local(): attended_all = lax.all_gather(attended_own, 'ctx', axis=0, tiled=True)]
    dot_general x23 -> x0, matrix products: 102 us -> none  [the longest x8 43.4 us: advance(): jnp.dot(query_rows, block_pair[0].T, preferred_element_type=jnp.float32)]
    psum x2 -> x0, blocking collectives: 62.4 us -> none  [the longest x1 41 us: local(): exp_total, target_logit = lax.psum((exp_part, target_part), ('ctx', 'tp'))]
    reduce_sum x14 -> x1, other arithmetic: 45.3 us -> 0.19 us  [local(): jnp.sum(jnp.where(member, token_logprob[None, :], 0.0), axis=1)]
    pmax x1 -> x0, blocking collectives: 39.3 us -> none  [local(): global_max = lax.pmax(local_max, ('ctx', 'tp'))]
    all_to_all x3 -> x0, waiting for transfers between devices: 25.4 us -> none  [the longest x1 22.5 us: local(): lax.all_to_all(part_weighted[None].astype(jnp.bfloat16), 'ctx', split_axi...]
    reduce_scatter x1 -> x0, waiting for transfers between devices: 20.5 us -> none  [local(): lax.psum_scatter(jnp.dot(attended_all, out_weight, preferred_element_type...]
  transfers between devices with their start and end apart: 8 -> 0, of which waited for: 7 -> 0; matrix products, arithmetic and copies ran while one was open for 4% -> 0% of each run, Pallas kernels for 0% -> 0%
where the time goes in v1:
time: 210 us; the launch traced here: 209 us
  Pallas kernels  200 us (95%)
  local copies, waits for them, and re-layouts  7.4 us (4%)
    pallas_call x1, Pallas kernels, local(): pl.pallas_call(functools.partial(kernel, n_ctx, n_tp, slots, chunk), out_...  200 us
    unnamed x10, local copies, waits for them, and re-layouts  4.27 us

profile of v1, /device:TPU:0, one launch (start us, length us, event | category | flops | bytes accessed | tf_op | source)
XLA Modules:
  0.0 208.8 jit_solution(4665326056501797927)
XLA Ops:
  0.6 0.0 copy-start
  0.6 0.0 copy-start.1
  0.7 0.0 copy-start.2
  0.7 4.1 %copy.15 = bf16[4096,256]{0,1:T(8,128)(2,1)} copy(bf16[4096,256]{1,0:T(8,128)(2,1)} %param.13) | data formatting | bytes 4194304 | tf_op args[2]
  4.8 0.0 copy-done
  4.8 0.1 copy.16
  4.9 0.6 pad_bitcast_fusion.fresh_value_ref
  5.6 0.0 copy-done.1
  5.6 0.6 pad.7.fresh_key_ref
  6.2 0.0 copy-done.2
  6.2 0.6 broadcast_in_dim.24.gain_ref
  6.8 0.0 copy-start.3
  6.8 199.9 %score_span.1 = f32[8,256]{1,0:T(8,128)} custom-call(bf16[32,2048]{1,0:T(8,128)(2,1)} %query_ref.1, bf16[4096,256]{1,0:T(8,128)(2,1)} %key_ref.1, bf16[256,4096]{1,0:T(8,128)(2,1)} %bitcast.12, bf16[128,256]{1,0:T(8,128)(2,1)} %pad.7.fresh_key_ref, bf16[256,128]{1,0:T(8,128)(2,1)} %pad_bitcast_fusion.fresh_value_ref, bf16[64,1024]{1,0:T(8,128)(2,1)} %residual_ref.1, ...), custom_call_target="tpu_custom_call" | custom-call | tf_op jit(solution)/shard_map/score_span/pallas_call | solution.py:472
  206.7 0.7 slice.3
  207.4 0.6 dynamic-slice_bitcast_fusion
  207.9 0.0 copy-done.3
  207.9 0.2 reduce-window.8
  208.1 0.2 select_reduce_fusion
  208.3 0.5 convert_divide_fusion
  (1 shorter events, 0.0 us)
Async XLA Ops:
  0.6 4.2 %copy-start = (bf16[32,256]{1,0:T(8,128)(2,1)S(1)}, bf16[32,256]{1,0:T(8,128)(2,1)}, u32[]{:S(2)}) copy-start(bf16[32,256]{1,0:T(8,128)(2,1)} %param.15) | copy-start | bytes 49156
  0.6 4.9 %copy-start.1 = (bf16[32,256]{1,0:T(8,128)(2,1)S(1)}, bf16[32,256]{1,0:T(8,128)(2,1)}, u32[]{:S(2)}) copy-start(bf16[32,256]{1,0:T(8,128)(2,1)} %param.14) | copy-start | bytes 49156
  0.7 5.5 %copy-start.2 = (bf16[1024]{0:T(1024)(128)(2,1)S(1)}, bf16[1024]{0:T(1024)(128)(2,1)}, u32[]{:S(2)}) copy-start(bf16[1024]{0:T(1024)(128)(2,1)} %param.18) | copy-start | bytes 6148
  6.8 201.2 %copy-start.3 = (s32[4]{0:T(128)S(1)}, s32[4]{0:T(128)}, u32[]{:S(2)}) copy-start(s32[4]{0:T(128)} %param.21) | copy-start | bytes 52
